TPU v7x, 32 devices: a whole 2x2x4 slice. The times are simulated.
32 devices in a mesh: dp: 16 (over z, y, core), seq: 2 (over x).
Axes of the slice: x: 2, y: 2, z: 4, core: 2. Of those that a mesh axis runs over, the one named last changes fastest.
Arguments:
- tile_feats: bfloat16 [8192, 2048], P('dp'), may hold values from -6 to 6
- tile_pos: int32 [16, 512], P('dp'), may hold values from -1 to 511, as said below
- slide_count: int32 [16], P('dp'), may hold values from 128 to 512, as said below
- w_proj: bfloat16 [2048, 768], P(None, 'seq'), may hold values from -0.125 to 0.125
- emb_grad: bfloat16 [16, 512, 768], P('dp', 'seq'), may hold values from -6 to 6
- ln_gain: float32 [768], replicated, may hold values from 0.25 to 1.75
- w_qkv: bfloat16 [768, 2304], P('dp'), may hold values from -1.5 to 1.5
- w_out: bfloat16 [768, 768], P('dp'), may hold values from -0.21875 to 0.21875
Outputs:
- slide_emb: bfloat16 [16, 512, 768], P('dp', 'seq')
- attn_branch: bfloat16 [16, 512, 768], P('dp', 'seq')
- proj_grad: float32 [2048, 768], P(None, 'seq')
Inputs may be any that keep to these rules, and one draw needn't show every extreme that they name: `tile_pos`: slot j of a row belongs to slide j // 32. Each position below a slide's slide_count is held by exactly one slot of that slide over all rows; all other slots hold -1. `slide_count`: some slide is full.
All inputs are finite; a program needn't handle non-finite values.
Results may differ from a plain program's by a relative error of at most 0.017.
The roundings to bfloat16 on the way count: a program that leaves them out, or rounds other values in their place, can miss the bound.
Values may be sent and summed in bfloat16 or wider, within the bound.
A program may use at most 128 MiB of HBM per device.

v0:
```python
import jax
import jax.numpy as jnp
from jax import lax
from jax.sharding import PartitionSpec as P

D = 768
HEAD_COUNT = 12
HEAD_WIDTH = 64
DILATION_STEP = 4
NEGATIVE = -1e30
EPSILON = 1e-05


def selection_shift(values, heads, dilation):
    length = values.shape[1]
    rest = values.shape[2:]
    shaped = values.reshape((heads, length // dilation, dilation) + rest)
    return jnp.stack(
        [shaped[head_number, :, head_number % dilation] for head_number in range(heads)]
    )


def insertion_shift(values, chosen, heads, dilation):
    length = values.shape[1]
    rest = values.shape[2:]
    shaped = values.reshape((heads, length // dilation, dilation) + rest)
    shift_amounts = jnp.arange(heads, dtype=jnp.int32) % dilation
    select = jnp.arange(dilation, dtype=jnp.int32)[None, :] == shift_amounts[:, None]
    select = select.reshape((heads, 1, dilation) + (1,) * len(rest))
    merged = jnp.where(select, chosen[:, :, None], shaped)
    return merged.reshape(values.shape)


def local(tile_feats, tile_pos, slide_count, w_proj, emb_grad, ln_gain, w_qkv, w_out):
    seq_count = lax.axis_size("seq")
    seq_index = lax.axis_index("seq")
    slot_rows = tile_feats.shape[0]
    nearby_length = emb_grad.shape[1]
    slide_len = nearby_length * seq_count
    inner = HEAD_COUNT * HEAD_WIDTH
    scale = HEAD_WIDTH ** (-0.5)
    tile_count = slide_count[0]
    emb_part = jnp.dot(tile_feats, w_proj, preferred_element_type=jnp.float32).astype(jnp.bfloat16)
    feature_part = emb_part.shape[1]
    positions = tile_pos.reshape(slot_rows)
    arrived, arrived_pos = (
        lax.all_to_all(emb_part, "dp", split_axis=0, concat_axis=0, tiled=True),
        lax.all_to_all(positions, "dp", split_axis=0, concat_axis=0, tiled=True),
    )
    target = jnp.where(arrived_pos >= 0, arrived_pos, slide_len).astype(jnp.int32)
    slide_rows = (
        jnp.zeros((slide_len + 1, feature_part), jnp.bfloat16).at[target].set(arrived)[:slide_len]
    )
    local_emb = lax.all_to_all(slide_rows, "seq", split_axis=0, concat_axis=1, tiled=True)
    widened = local_emb.astype(jnp.float32)
    center = jnp.mean(widened, axis=-1, keepdims=True)
    spread = jnp.mean(jnp.square(widened - center), axis=-1, keepdims=True)
    normed = ((widened - center) * lax.rsqrt(spread + EPSILON) * ln_gain).astype(jnp.bfloat16)
    columns = normed
    projected = jnp.dot(
        columns, lax.all_gather(w_qkv, "dp", axis=0, tiled=True), preferred_element_type=jnp.float32
    )
    projected = projected.astype(jnp.bfloat16)
    query_rows = projected[:, :inner].reshape(nearby_length, HEAD_COUNT, HEAD_WIDTH)
    key_matrix = projected[:, inner : 2 * inner].reshape(nearby_length, HEAD_COUNT, HEAD_WIDTH)
    value_matrix = projected[:, 2 * inner :].reshape(nearby_length, HEAD_COUNT, HEAD_WIDTH)
    sequence_position = seq_index * nearby_length + jnp.arange(nearby_length, dtype=jnp.int32)
    occupied = sequence_position < tile_count
    shift_amounts = jnp.arange(HEAD_COUNT, dtype=jnp.int32) % DILATION_STEP
    local_scores = (
        jnp.einsum("qhd,khd->hqk", query_rows, key_matrix, preferred_element_type=jnp.float32)
        * scale
    )
    local_ok = jnp.broadcast_to(occupied[None, None, :], local_scores.shape)
    nearby_maximum = jnp.max(jnp.where(local_ok, local_scores, NEGATIVE), axis=-1)
    local_weight = jnp.where(local_ok, jnp.exp(local_scores - nearby_maximum[..., None]), 0.0)
    nearby_sum = jnp.sum(local_weight, axis=-1)
    nearby_accumulator = jnp.einsum("hqk,khd->hqd", local_weight, value_matrix.astype(jnp.float32))
    stepped_queries = query_rows.reshape(
        nearby_length // DILATION_STEP, DILATION_STEP, HEAD_COUNT, HEAD_WIDTH
    )
    selected_query = jnp.stack(
        [
            stepped_queries[:, head_number % DILATION_STEP, head_number, :]
            for head_number in range(HEAD_COUNT)
        ]
    )
    key_value = jnp.concatenate([key_matrix, value_matrix], axis=-1)
    flat_rows = key_value.reshape(nearby_length, HEAD_COUNT * 2 * HEAD_WIDTH)
    portion = lax.all_gather(flat_rows, "seq", axis=0, tiled=True)
    row_counts = portion.shape[0]
    head_split = (row_counts + DILATION_STEP - 1) // DILATION_STEP
    shaped = portion.reshape(row_counts, HEAD_COUNT, 2 * HEAD_WIDTH)
    leading_index = shift_amounts % DILATION_STEP
    index_of_row = (
        leading_index[:, None] + DILATION_STEP * jnp.arange(head_split, dtype=jnp.int32)[None, :]
    )
    inside = index_of_row < row_counts
    safe_index = jnp.minimum(index_of_row, row_counts - 1)
    head_index = jnp.arange(HEAD_COUNT, dtype=jnp.int32)[:, None]
    chosen = shaped[safe_index, head_index, :]
    key_ok = inside & (index_of_row < tile_count)
    previous_maximum = selection_shift(nearby_maximum, HEAD_COUNT, DILATION_STEP)
    previous_sum = selection_shift(nearby_sum, HEAD_COUNT, DILATION_STEP)
    previous_accumulator = selection_shift(nearby_accumulator, HEAD_COUNT, DILATION_STEP)
    far_scores = (
        jnp.einsum(
            "hqd,hkd->hqk",
            selected_query,
            chosen[..., :HEAD_WIDTH],
            preferred_element_type=jnp.float32,
        )
        * scale
    )
    usable = jnp.broadcast_to(key_ok[:, None, :], far_scores.shape)
    new_max = jnp.maximum(
        previous_maximum, jnp.max(jnp.where(usable, far_scores, NEGATIVE), axis=-1)
    )
    far_weight = jnp.where(usable, jnp.exp(far_scores - new_max[..., None]), 0.0)
    rescale = jnp.exp(previous_maximum - new_max)
    updated_sum = previous_sum * rescale + jnp.sum(far_weight, axis=-1)
    updated_accumulator = previous_accumulator * rescale[..., None] + jnp.einsum(
        "hqk,hkd->hqd", far_weight, chosen[..., HEAD_WIDTH:].astype(jnp.float32)
    )
    complete_sum = insertion_shift(nearby_sum, updated_sum, HEAD_COUNT, DILATION_STEP)
    complete_accumulator = insertion_shift(
        nearby_accumulator, updated_accumulator, HEAD_COUNT, DILATION_STEP
    )
    safe_total = jnp.where(occupied[None, :], complete_sum, 1.0)
    context = jnp.where(occupied[None, :, None], complete_accumulator / safe_total[..., None], 0.0)
    context = context.transpose(1, 0, 2).reshape(nearby_length, inner).astype(jnp.bfloat16)
    columns = context
    branch_out = jnp.dot(
        columns, lax.all_gather(w_out, "dp", axis=0, tiled=True), preferred_element_type=jnp.float32
    )
    attn_branch = branch_out.astype(jnp.bfloat16)
    returned_grad = lax.all_to_all(
        emb_grad.reshape(nearby_length, D), "seq", split_axis=1, concat_axis=0, tiled=True
    )
    padded_grad = jnp.concatenate(
        [returned_grad, jnp.zeros((1, feature_part), jnp.bfloat16)], axis=0
    )
    picked_grad = padded_grad[target]
    slot_grad = lax.all_to_all(picked_grad, "dp", split_axis=0, concat_axis=0, tiled=True)
    grad_part = lax.dot_general(
        tile_feats, slot_grad, (((0,), (0,)), ((), ())), preferred_element_type=jnp.float32
    )
    proj_grad = lax.psum(grad_part, "dp")
    return (local_emb[None], attn_branch[None], proj_grad)


def solution(mesh):
    in_specs = (
        P("dp", None),
        P("dp", None),
        P("dp"),
        P(None, "seq"),
        P("dp", "seq", None),
        P(),
        P("dp", None),
        P("dp", None),
    )
    out_specs = (P("dp", "seq", None), P("dp", "seq", None), P(None, "seq"))
    return jax.shard_map(local, mesh=mesh, in_specs=in_specs, out_specs=out_specs, check_vma=False)
```

profile of v0, /device:TPU:0, one launch (start us, length us, event | category | flops | bytes accessed | tf_op | source)
XLA Modules:
  0.0 267.3 jit_solution(15064173347911541342)
XLA Ops:
  10.5 7.4 %all-to-all-start = ((s32[16,32,1]{1,2,0:T(1,128)}), s32[16,32,1]{1,2,0:T(1,128)S(1)}, u32[]{:S(2)}, u32[]{:S(2)}) async-start(s32[16,32,1]{1,2,0:T(1,128)} %all_to_all.50), calls=%async_computation | async-start | bytes 16384 | tf_op jit(solution)/shard_map/all_to_all | solution.py:48
  17.9 3.5 %convolution_convert_fusion.2 = bf16[512,384]{1,0:T(8,128)(2,1)} fusion(bf16[512,2048]{1,0:T(8,128)(2,1)S(1)} %copy-done, bf16[2048,384]{1,0:T(8,128)(2,1)} %param.11), kind=kOutput, calls=%fused_computation.14 | convolution fusion | flops 805502976 | bytes 4063232 | tf_op jit(solution)/shard_map/dot_general | solution.py:43
  21.3 2.9 %all-to-all-done = s32[16,32,1]{1,2,0:T(1,128)S(1)} async-done(((s32[16,32,1]{1,2,0:T(1,128)}), s32[16,32,1]{1,2,0:T(1,128)S(1)}, u32[]{:S(2)}, u32[]{:S(2)}) %all-to-all-start) | async-done | bytes 2080 | tf_op jit(solution)/shard_map/all_to_all | solution.py:48
  24.2 3.6 %all-to-all-start.1 = ((bf16[16,32,384]{2,1,0:T(8,128)(2,1)}), bf16[16,32,384]{2,1,0:T(8,128)(2,1)S(1)}, u32[]{:S(2)}, u32[]{:S(2)}) async-start(bf16[16,32,384]{2,1,0:T(8,128)(2,1)} %bitcast.1), calls=%async_computation.1 | async-start | bytes 786432 | tf_op jit(solution)/shard_map/all_to_all | solution.py:47
  29.4 12.1 %all-to-all-done.1 = bf16[16,32,384]{2,1,0:T(8,128)(2,1)S(1)} async-done(((bf16[16,32,384]{2,1,0:T(8,128)(2,1)}), bf16[16,32,384]{2,1,0:T(8,128)(2,1)S(1)}, u32[]{:S(2)}, u32[]{:S(2)}) %all-to-all-start.1) | async-done | bytes 393248 | tf_op jit(solution)/shard_map/all_to_all | solution.py:47
  42.2 3.5 %all-to-all-start.3 = ((bf16[256,2,384]{2,0,1:T(8,128)(2,1)}), bf16[256,2,384]{2,0,1:T(8,128)(2,1)S(1)}, u32[]{:S(2)}, u32[]{:S(2)}) async-start(bf16[256,2,384]{2,0,1:T(8,128)(2,1)} %copy.164), calls=%async_computation.3 | async-start | bytes 786432 | tf_op jit(solution)/shard_map/all_to_all | solution.py:137
  45.7 2.9 %scatter_custom_fusion = bf16[513,384]{1,0:T(8,128)(2,1)S(1)} fusion(s32[512]{0:T(512)S(1)} %bitcast.199, bf16[512,384]{1,0:T(8,128)(2,1)} %bitcast.185, bf16[]{:T(256)} %constant.24.clone.1), kind=kCustom, calls=%fused_computation.31 | custom fusion | bytes 394496 | tf_op jit(solution)/shard_map/scatter | solution.py:52
  49.4 3.2 %all-to-all-done.3 = bf16[256,2,384]{2,0,1:T(8,128)(2,1)S(1)} async-done(((bf16[256,2,384]{2,0,1:T(8,128)(2,1)}), bf16[256,2,384]{2,0,1:T(8,128)(2,1)S(1)}, u32[]{:S(2)}, u32[]{:S(2)}) %all-to-all-start.3) | async-done | bytes 393248 | tf_op jit(solution)/shard_map/all_to_all | solution.py:137
  52.6 3.5 %all-to-all-start.2 = ((bf16[2,256,384]{2,1,0:T(8,128)(2,1)}), bf16[2,256,384]{2,1,0:T(8,128)(2,1)S(1)}, u32[]{:S(2)}, u32[]{:S(2)}) async-start(bf16[2,256,384]{2,1,0:T(8,128)(2,1)} %bitcast.3), calls=%async_computation.2 | async-start | bytes 786432 | tf_op jit(solution)/shard_map/all_to_all | solution.py:54
  56.1 2.6 gather_fusion.1
  58.7 3.5 %all-to-all-done.2 = bf16[2,256,384]{2,1,0:T(8,128)(2,1)S(1)} async-done(((bf16[2,256,384]{2,1,0:T(8,128)(2,1)}), bf16[2,256,384]{2,1,0:T(8,128)(2,1)S(1)}, u32[]{:S(2)}, u32[]{:S(2)}) %all-to-all-start.2) | async-done | bytes 393248 | tf_op jit(solution)/shard_map/all_to_all | solution.py:54
  62.1 4.8 %all-to-all-start.4 = ((bf16[16,32,384]{2,1,0:T(8,128)(2,1)}), bf16[16,32,384]{2,1,0:T(8,128)(2,1)}, u32[]{:S(2)}, u32[]{:S(2)}) async-start(bf16[16,32,384]{2,1,0:T(8,128)(2,1)} %bitcast.50), calls=%async_computation.4 | async-start | bytes 786432 | tf_op jit(solution)/shard_map/all_to_all | solution.py:144
  69.3 9.9 %all-to-all-done.4 = bf16[16,32,384]{2,1,0:T(8,128)(2,1)} async-done(((bf16[16,32,384]{2,1,0:T(8,128)(2,1)}), bf16[16,32,384]{2,1,0:T(8,128)(2,1)}, u32[]{:S(2)}, u32[]{:S(2)}) %all-to-all-start.4) | async-done | bytes 393248 | tf_op jit(solution)/shard_map/all_to_all | solution.py:144
  79.2 3.7 %convolution_bitcast_fusion = f32[2048,384]{0,1:T(8,128)} fusion(bf16[512,384]{1,0:T(8,128)(2,1)} %bitcast.51, bf16[512,2048]{1,0:T(8,128)(2,1)S(1)} %copy-done), kind=kOutput, calls=%fused_computation.6 | convolution fusion | flops 805306368 | bytes 5636096 | tf_op jit(solution)/shard_map/dot_general | solution.py:145
  84.4 3.5 %convolution_convert_fusion = bf16[256,2304]{1,0:T(8,128)(2,1)S(1)} fusion(bf16[256,768]{0,1:T(8,128)(2,1)} %fusion.9, bf16[768,2304]{1,0:T(8,128)(2,1)} %all-gather.4.cloned.1.call-done), kind=kOutput, calls=%fused_computation.3 | convolution fusion | flops 906559488 | bytes 5111808 | tf_op jit(solution)/shard_map/dot_general | solution.py:60
  97.2 87.1 %all-reduce.3.cloned.1.call-done = f32[2048,384]{0,1:T(8,128)} async-done(((f32[2048,384]{0,1:T(8,128)}), f32[2048,384]{0,1:T(8,128)}) %all-reduce.3.cloned.1.call-update) | async-done | bytes 3145744 | tf_op jit(solution)/shard_map/psum | solution.py:148
  184.4 3.5 %copy.166 = f32[2048,384]{1,0:T(8,128)} copy(f32[2048,384]{0,1:T(8,128)} %all-reduce.3.cloned.1.call-done) | data formatting | bytes 6291456
  192.1 2.8 %fusion.1 = f32[12,256,64]{1,2,0:T(8,128)S(1)} fusion(bf16[256,12,64]{0,2,1:T(8,128)(2,1)} %bitcast.181, f32[12,256,256]{1,2,0:T(8,128)} %get-tuple-element.69, f32[12,256]{1,0:T(8,128)S(1)} %get-tuple-element.68, pred[256]{0:T(512)(128)(4,1)S(1)} %add_compare_fusion.2), kind=kOutput, calls=%fused_computation.8 | convolution fusion | flops 103022592 | bytes 4337920 | tf_op jit(solution)/shard_map/hqk,khd->hqd/dot_general | solution.py:78
  200.7 2.6 fusion.29
  203.3 3.4 %slice_reduce_fusion.12 = (f32[64]{0:T(128)S(1)}, f32[64]{0:T(128)S(1)}, f32[64]{0:T(128)S(1)}, f32[64]{0:T(128)}, f32[64]{0:T(128)}, /*index=5*/f32[64]{0:T(128...) fusion(f32[12,64,4]{0,2,1:T(4,128)S(1)} %bitcast.175), kind=kLoop, calls=%fused_computation.72 | loop fusion | bytes 6144 | tf_op jit(solution)/shard_map/slice | solution.py:19
  206.8 3.4 %slice_reduce_fusion = (f32[64]{0:T(128)}, f32[64]{0:T(128)}, f32[64]{0:T(128)}, f32[64]{0:T(128)}, f32[64]{0:T(128)}, /*index=5*/f32[64]{0:T(128)}, f32[64]{0:T...) fusion(f32[12,64,4]{0,2,1:T(4,128)S(1)} %bitcast.176), kind=kLoop, calls=%fused_computation.60 | loop fusion | bytes 6144 | tf_op jit(solution)/shard_map/slice | solution.py:19
  229.7 2.6 copy.156
  232.3 17.9 %gather_fusion = bf16[1536,128]{1,0:T(8,128)(2,1)S(1)} fusion(bf16[512,12,128]{2,0,1:T(8,128)(2,1)} %copy.156, s32[1536]{0:T(1024)S(1)} %fusion.21), kind=kCustom, calls=%fused_computation | custom fusion | bytes 798720 | tf_op jit(solution)/shard_map/gather | solution.py:101
  253.9 2.8 %copy.159 = f32[12,256,64]{1,2,0:T(8,128)} copy(f32[12,256,64]{2,1,0:T(8,128)} %bitcast.168) | data formatting | bytes 1572864 | tf_op jit(solution)/shard_map/jit(_where)/broadcast_in_dim | solution.py:30
  (100 shorter events, 56.4 us)
Async XLA Ops:
  7.2 10.7 %copy-start = (bf16[512,2048]{1,0:T(8,128)(2,1)S(1)}, bf16[512,2048]{1,0:T(8,128)(2,1)}, u32[]{:S(2)}) copy-start(bf16[512,2048]{1,0:T(8,128)(2,1)} %param.8) | copy-start | bytes 6291460
  7.2 77.3 %all-gather.4.cloned.1.call-start = ((), (), s32[]{:S(2)}) async-start(), calls=%async_computation.5 | async-start | bytes 3760128 | tf_op jit(solution)/shard_map/all_gather | solution.py:61
  10.5 13.7 %all-to-all-start = ((s32[16,32,1]{1,2,0:T(1,128)}), s32[16,32,1]{1,2,0:T(1,128)S(1)}, u32[]{:S(2)}, u32[]{:S(2)}) async-start(s32[16,32,1]{1,2,0:T(1,128)} %all_to_all.50), calls=%async_computation | async-start | bytes 16384 | tf_op jit(solution)/shard_map/all_to_all | solution.py:48
  17.9 9.9 %copy-start.2 = (bf16[1,256,768]{2,1,0:T(8,128)(2,1)S(1)}, bf16[1,256,768]{2,1,0:T(8,128)(2,1)}, u32[]{:S(2)}) copy-start(bf16[1,256,768]{2,1,0:T(8,128)(2,1)} %param.12) | copy-start | bytes 1179652
  24.2 17.3 %all-to-all-start.1 = ((bf16[16,32,384]{2,1,0:T(8,128)(2,1)}), bf16[16,32,384]{2,1,0:T(8,128)(2,1)S(1)}, u32[]{:S(2)}, u32[]{:S(2)}) async-start(bf16[16,32,384]{2,1,0:T(8,128)(2,1)} %bitcast.1), calls=%async_computation.1 | async-start | bytes 786432 | tf_op jit(solution)/shard_map/all_to_all | solution.py:47
  41.5 0.7 copy-start.3
  42.2 10.3 %all-to-all-start.3 = ((bf16[256,2,384]{2,0,1:T(8,128)(2,1)}), bf16[256,2,384]{2,0,1:T(8,128)(2,1)S(1)}, u32[]{:S(2)}, u32[]{:S(2)}) async-start(bf16[256,2,384]{2,0,1:T(8,128)(2,1)} %copy.164), calls=%async_computation.3 | async-start | bytes 786432 | tf_op jit(solution)/shard_map/all_to_all | solution.py:137
  52.6 9.6 %all-to-all-start.2 = ((bf16[2,256,384]{2,1,0:T(8,128)(2,1)}), bf16[2,256,384]{2,1,0:T(8,128)(2,1)S(1)}, u32[]{:S(2)}, u32[]{:S(2)}) async-start(bf16[2,256,384]{2,1,0:T(8,128)(2,1)} %bitcast.3), calls=%async_computation.2 | async-start | bytes 786432 | tf_op jit(solution)/shard_map/all_to_all | solution.py:54
  62.1 17.0 %all-to-all-start.4 = ((bf16[16,32,384]{2,1,0:T(8,128)(2,1)}), bf16[16,32,384]{2,1,0:T(8,128)(2,1)}, u32[]{:S(2)}, u32[]{:S(2)}) async-start(bf16[16,32,384]{2,1,0:T(8,128)(2,1)} %bitcast.50), calls=%async_computation.4 | async-start | bytes 786432 | tf_op jit(solution)/shard_map/all_to_all | solution.py:144
  66.9 117.5 %all-reduce.3.cloned.1.call-start = ((), (), s32[]{:S(2)}) async-start(), calls=%async_computation.8 | async-start | bytes 6291456 | tf_op jit(solution)/shard_map/psum | solution.py:148
  82.8 0.7 copy-start.4
  82.9 146.8 %all-gather.6.cloned.1.call-start = ((), (), s32[]{:S(2)}) async-start(), calls=%async_computation.6 | async-start | bytes 2359296 | tf_op jit(solution)/shard_map/all_gather | solution.py:90
  92.8 165.5 %all-gather.8.cloned.1.call-start = ((), (), s32[]{:S(2)}) async-start(), calls=%async_computation.7 | async-start | bytes 1253376 | tf_op jit(solution)/shard_map/all_gather | solution.py:134
  192.1 3.1 %copy-start.1 = (f32[12,256,256]{1,2,0:T(8,128)S(1)}, f32[12,256,256]{1,2,0:T(8,128)}, u32[]{:S(2)}) copy-start(f32[12,256,256]{1,2,0:T(8,128)} %get-tuple-element.69) | copy-start | bytes 9437188
Sparse Core Ops, SparseCore 0:
  10.3 52.3 all-gather.3
  83.0 101.3 all-reduce.2
  185.9 26.3 all-gather.5
  214.4 38.3 all-gather.7
where the time goes:
time: 269 us; the launch traced here: 267 us
  waiting for transfers between devices  120 us (45%)
  local copies, waits for them, and re-layouts  81 us (30%)
  starting transfers between devices  23 us (9%)
  matrix products  20.2 us (8%)
  between operations  14.7 us (5%)
  other arithmetic  8.78 us (3%)
    psum x1, waiting for transfers between devices, local(): proj_grad = lax.psum(grad_part, 'dp')  87.1 us
    unnamed x35, local copies, waits for them, and re-layouts  24 us
    gather x1, local copies, waits for them, and re-layouts, local(): chosen = shaped[safe_index, head_index, :]  17.9 us
    all_to_all x1, waiting for transfers between devices, local(): lax.all_to_all(emb_part, 'dp', split_axis=0, concat_axis=0, tiled=True)  12.1 us
    all_to_all x1, waiting for transfers between devices, local(): lax.all_to_all(picked_grad, 'dp', split_axis=0, concat_axis=0, tiled=True)  9.87 us
    slice x3, local copies, waits for them, and re-layouts, selection_shift(): shaped[head_number, :, head_number % dilation]  9.23 us
    all_to_all x1, starting transfers between devices, local(): lax.all_to_all(positions, 'dp', split_axis=0, concat_axis=0, tiled=True)  7.39 us
  transfers between devices with their start and end apart: 9, of which 6 were waited for; matrix products, arithmetic and copies ran while one was open for 39% of the time, Pallas kernels for 0%

commit v1 on v0

--- a/solution.py
+++ b/solution.py
@@ -145,7 +145,11 @@
     grad_part = lax.dot_general(
         tile_feats, slot_grad, (((0,), (0,)), ((), ())), preferred_element_type=jnp.float32
     )
-    proj_grad = lax.psum(grad_part, "dp")
+    proj_grad = grad_part
+    for hop in (1, 2, 4, 8):
+        proj_grad = proj_grad + lax.ppermute(
+            proj_grad, "dp", [(dev, dev ^ hop) for dev in range(16)]
+        )
     return (local_emb[None], attn_branch[None], proj_grad)
 
 

time: 269 us -> 405 us (1.51)
  waiting for transfers between devices: 120 us -> 251 us
  local copies, waits for them, and re-layouts: 81 us -> 58.8 us
  other arithmetic: 8.78 us -> 25.7 us
  blocking collectives: 0 us -> 9.53 us
    ppermute x0 -> x4, waiting for transfers between devices: none -> 216 us  [local(): lax.ppermute(proj_grad, 'dp', [(dev, dev ^ hop) for dev in range(16)])]
    psum x1 -> x0, waiting for transfers between devices: 87.1 us -> none  [local(): proj_grad = lax.psum(grad_part, 'dp')]
    add x0 -> x4, other arithmetic: none -> 18 us  [local(): proj_grad + lax.ppermute(proj_grad, 'dp', [(dev, dev ^ hop) for dev in ra...]
    gather x1, local copies, waits for them, and re-layouts: 17.9 us -> 8.07 us  [local(): chosen = shaped[safe_index, head_index, :]]
    all_to_all x0 -> x1, blocking collectives: none -> 9.53 us  [local(): lax.all_to_all(slide_rows, 'seq', split_axis=0, concat_axis=1, tiled=True)]
    all_to_all x1, waiting for transfers between devices: 9.87 us -> 15.3 us  [local(): lax.all_to_all(picked_grad, 'dp', split_axis=0, concat_axis=0, tiled=True)]
    unnamed x35 -> x45, local copies, waits for them, and re-layouts: 24 us -> 20.1 us
  transfers between devices with their start and end apart: 9 -> 11, of which waited for: 6 -> 7; matrix products, arithmetic and copies ran while one was open for 39% -> 23% of each run, Pallas kernels for 0% -> 0%
where the time goes in v1:
time: 405 us; the launch traced here: 404 us
  waiting for transfers between devices  251 us (62%)
  local copies, waits for them, and re-layouts  58.8 us (15%)
  other arithmetic  25.7 us (6%)
  starting transfers between devices  25.4 us (6%)
  matrix products  18.1 us (4%)
  between operations  14.9 us (4%)
  blocking collectives  9.53 us (2%)
    ppermute x4, waiting for transfers between devices, local(): lax.ppermute(proj_grad, 'dp', [(dev, dev ^ hop) for dev in range(16)])  216 us
    unnamed x45, local copies, waits for them, and re-layouts  20.1 us
    add x4, other arithmetic, local(): proj_grad + lax.ppermute(proj_grad, 'dp', [(dev, dev ^ hop) for dev in ra...  18 us
    all_to_all x1, waiting for transfers between devices, local(): lax.all_to_all(picked_grad, 'dp', split_axis=0, concat_axis=0, tiled=True)  15.3 us
    all_to_all x1, blocking collectives, local(): lax.all_to_all(slide_rows, 'seq', split_axis=0, concat_axis=1, tiled=True)  9.53 us
    all_to_all x1, waiting for transfers between devices, local(): lax.all_to_all(emb_part, 'dp', split_axis=0, concat_axis=0, tiled=True)  9.07 us
    slice x3, local copies, waits for them, and re-layouts, selection_shift(): shaped[head_number, :, head_number % dilation]  8.7 us
  transfers between devices with their start and end apart: 11, of which 7 were waited for; matrix products, arithmetic and copies ran while one was open for 23% of the time, Pallas kernels for 0%

profile of v1, /device:TPU:0, one launch (start us, length us, event | category | flops | bytes accessed | tf_op | source)
XLA Modules:
  0.0 403.7 jit_solution(5550719582075508399)
XLA Ops:
  10.5 7.4 %all-to-all-start = ((s32[16,32,1]{1,2,0:T(1,128)}), s32[16,32,1]{1,2,0:T(1,128)S(1)}, u32[]{:S(2)}, u32[]{:S(2)}) async-start(s32[16,32,1]{1,2,0:T(1,128)} %all_to_all.50), calls=%async_computation | async-start | bytes 16384 | tf_op jit(solution)/shard_map/all_to_all | solution.py:48
  19.7 4.4 %all-to-all-done = s32[16,32,1]{1,2,0:T(1,128)S(1)} async-done(((s32[16,32,1]{1,2,0:T(1,128)}), s32[16,32,1]{1,2,0:T(1,128)S(1)}, u32[]{:S(2)}, u32[]{:S(2)}) %all-to-all-start) | async-done | bytes 2080 | tf_op jit(solution)/shard_map/all_to_all | solution.py:48
  24.2 3.5 all-to-all-start.3
  28.4 6.0 %all-to-all-done.3 = bf16[256,2,384]{2,0,1:T(8,128)(2,1)S(1)} async-done(((bf16[256,2,384]{2,0,1:T(8,128)(2,1)}), bf16[256,2,384]{2,0,1:T(8,128)(2,1)S(1)}, u32[]{:S(2)}, u32[]{:S(2)}) %all-to-all-start.3) | async-done | bytes 393248 | tf_op jit(solution)/shard_map/all_to_all | solution.py:137
  37.1 3.6 all-to-all-start.4
  40.7 3.4 convolution_convert_fusion.2
  44.1 15.3 %all-to-all-done.4 = bf16[16,32,384]{2,1,0:T(8,128)(2,1)S(1)} async-done(((bf16[16,32,384]{2,1,0:T(8,128)(2,1)}), bf16[16,32,384]{2,1,0:T(8,128)(2,1)S(1)}, u32[]{:S(2)}, u32[]{:S(2)}) %all-to-all-start.4) | async-done | bytes 393248 | tf_op jit(solution)/shard_map/all_to_all | solution.py:144
  59.4 7.0 %all-to-all-start.1 = ((bf16[16,32,384]{2,1,0:T(8,128)(2,1)}), bf16[16,32,384]{2,1,0:T(8,128)(2,1)S(1)}, u32[]{:S(2)}, u32[]{:S(2)}) async-start(bf16[16,32,384]{2,1,0:T(8,128)(2,1)} %bitcast.1), calls=%async_computation.1 | async-start | bytes 786432 | tf_op jit(solution)/shard_map/all_to_all | solution.py:47
  66.5 2.7 convolution_bitcast_fusion
  69.6 9.1 %all-to-all-done.1 = bf16[16,32,384]{2,1,0:T(8,128)(2,1)S(1)} async-done(((bf16[16,32,384]{2,1,0:T(8,128)(2,1)}), bf16[16,32,384]{2,1,0:T(8,128)(2,1)S(1)}, u32[]{:S(2)}, u32[]{:S(2)}) %all-to-all-start.1) | async-done | bytes 393248 | tf_op jit(solution)/shard_map/all_to_all | solution.py:47
  81.1 9.5 %all_to_all.71 = bf16[2,256,384]{2,1,0:T(8,128)(2,1)S(1)} all-to-all(bf16[2,256,384]{2,1,0:T(8,128)(2,1)S(1)} %bitcast.179), channel_id=1, replica_groups=mesh['dp'=16,'seq'=2] {'seq'}, dimensions={0} | all-to-all | bytes 786432 | tf_op jit(solution)/shard_map/all_to_all | solution.py:54
  91.6 3.1 convolution_convert_fusion
  96.5 5.2 %add.164 = f32[2048,384]{0,1:T(8,128)} add(f32[2048,384]{0,1:T(8,128)} %convolution_bitcast_fusion, f32[2048,384]{0,1:T(8,128)} %collective-permute-done) | non-fusion elementwise | flops 786432 | bytes 9437184 | tf_op jit(solution)/shard_map/add | solution.py:150
  111.2 2.7 copy.130
  116.0 59.3 %collective-permute-done.1 = f32[2048,384]{0,1:T(8,128)} collective-permute-done((f32[2048,384]{0,1:T(8,128)}, f32[2048,384]{0,1:T(8,128)}, u32[]{:S(2)}, u32[]{:S(2)}) %collective-permute-start.1) | collective-permute-done | bytes 3145760 | tf_op jit(solution)/shard_map/ppermute | solution.py:150
  175.3 3.3 add.165
  199.9 2.8 slice_reduce_fusion.12
  202.7 3.4 slice_reduce_fusion
  208.0 39.6 %collective-permute-done.2 = f32[2048,384]{0,1:T(8,128)} collective-permute-done((f32[2048,384]{0,1:T(8,128)S(1)}, f32[2048,384]{0,1:T(8,128)}, u32[]{:S(2)}, u32[]{:S(2)}) %collective-permute-start.2) | collective-permute-done | bytes 3145760 | tf_op jit(solution)/shard_map/ppermute | solution.py:150
  247.7 4.0 %add.166 = f32[2048,384]{0,1:T(8,128)} add(f32[2048,384]{0,1:T(8,128)S(1)} %add.165, f32[2048,384]{0,1:T(8,128)} %collective-permute-done.2) | non-fusion elementwise | flops 786432 | bytes 9437184 | tf_op jit(solution)/shard_map/add | solution.py:150
  256.6 8.1 %gather_fusion = bf16[1536,128]{1,0:T(8,128)(2,1)S(1)} fusion(bf16[512,12,128]{2,0,1:T(8,128)(2,1)S(1)} %copy.156, s32[1536]{0:T(1024)S(1)} %fusion.21), kind=kCustom, calls=%fused_computation | custom fusion | bytes 798720 | tf_op jit(solution)/shard_map/gather | solution.py:101
  271.5 116.8 %collective-permute-done.3 = f32[2048,384]{0,1:T(8,128)} collective-permute-done((f32[2048,384]{0,1:T(8,128)}, f32[2048,384]{0,1:T(8,128)}, u32[]{:S(2)}, u32[]{:S(2)}) %collective-permute-start.3) | collective-permute-done | bytes 3145760 | tf_op jit(solution)/shard_map/ppermute | solution.py:150
  388.3 5.4 %add.167 = f32[2048,384]{0,1:T(8,128)} add(f32[2048,384]{0,1:T(8,128)} %add.166, f32[2048,384]{0,1:T(8,128)} %collective-permute-done.3) | non-fusion elementwise | flops 786432 | bytes 9437184 | tf_op jit(solution)/shard_map/add | solution.py:150
  393.6 3.5 copy.166
  (118 shorter events, 59.6 us)
Async XLA Ops:
  7.2 33.5 %copy-start = (bf16[512,2048]{1,0:T(8,128)(2,1)S(1)}, bf16[512,2048]{1,0:T(8,128)(2,1)}, u32[]{:S(2)}) copy-start(bf16[512,2048]{1,0:T(8,128)(2,1)} %param.8) | copy-start | bytes 6291460
  7.2 84.4 %all-gather.4.cloned.1.call-start = ((), (), s32[]{:S(2)}) async-start(), calls=%async_computation.5 | async-start | bytes 3760128 | tf_op jit(solution)/shard_map/all_gather | solution.py:61
  10.5 13.7 %all-to-all-start = ((s32[16,32,1]{1,2,0:T(1,128)}), s32[16,32,1]{1,2,0:T(1,128)S(1)}, u32[]{:S(2)}, u32[]{:S(2)}) async-start(s32[16,32,1]{1,2,0:T(1,128)} %all_to_all.50), calls=%async_computation | async-start | bytes 16384 | tf_op jit(solution)/shard_map/all_to_all | solution.py:48
  24.2 10.3 %all-to-all-start.3 = ((bf16[256,2,384]{2,0,1:T(8,128)(2,1)}), bf16[256,2,384]{2,0,1:T(8,128)(2,1)S(1)}, u32[]{:S(2)}, u32[]{:S(2)}) async-start(bf16[256,2,384]{2,0,1:T(8,128)(2,1)} %copy.164), calls=%async_computation.3 | async-start | bytes 786432 | tf_op jit(solution)/shard_map/all_to_all | solution.py:137
  37.1 22.3 %all-to-all-start.4 = ((bf16[16,32,384]{2,1,0:T(8,128)(2,1)}), bf16[16,32,384]{2,1,0:T(8,128)(2,1)S(1)}, u32[]{:S(2)}, u32[]{:S(2)}) async-start(bf16[16,32,384]{2,1,0:T(8,128)(2,1)} %bitcast.50), calls=%async_computation.4 | async-start | bytes 786432 | tf_op jit(solution)/shard_map/all_to_all | solution.py:144
  59.4 19.2 %all-to-all-start.1 = ((bf16[16,32,384]{2,1,0:T(8,128)(2,1)}), bf16[16,32,384]{2,1,0:T(8,128)(2,1)S(1)}, u32[]{:S(2)}, u32[]{:S(2)}) async-start(bf16[16,32,384]{2,1,0:T(8,128)(2,1)} %bitcast.1), calls=%async_computation.1 | async-start | bytes 786432 | tf_op jit(solution)/shard_map/all_to_all | solution.py:47
  66.5 188.0 %all-gather.6.cloned.1.call-start = ((), (), s32[]{:S(2)}) async-start(), calls=%async_computation.6 | async-start | bytes 2359296 | tf_op jit(solution)/shard_map/all_gather | solution.py:90
  69.2 22.2 %copy-start.9 = (f32[768]{0:T(1024)S(1)}, f32[768]{0:T(1024)}, u32[]{:S(2)}) copy-start(f32[768]{0:T(1024)} %param.13) | copy-start | bytes 9220
  69.2 27.3 %collective-permute-start = (f32[2048,384]{0,1:T(8,128)}, f32[2048,384]{0,1:T(8,128)}, u32[]{:S(2)}, u32[]{:S(2)}) collective-permute-start(f32[2048,384]{0,1:T(8,128)} %convolution_bitcast_fusion), channel_id=1, source_target_pairs={{0,2},{2,0},{4,6},{6,4},{8,10},{10,8},{12,14},{14,12},{16,18},{18,... | collective-permute-start | bytes 9437192 | tf_op jit(solution)/shard_map/ppermute | solution.py:150
  95.0 6.7 %copy-start.4 = (bf16[256,768]{0,1:T(8,128)(2,1)}, bf16[256,768]{0,1:T(8,128)(2,1)S(1)}, u32[]{:S(2)}) copy-start(bf16[256,768]{0,1:T(8,128)(2,1)S(1)} %copy.128) | copy-start | bytes 1179652
  95.2 11.0 %copy-start.2 = (bf16[256,768]{0,1:T(8,128)(2,1)}, bf16[256,768]{0,1:T(8,128)(2,1)S(1)}, u32[]{:S(2)}) copy-start(bf16[256,768]{0,1:T(8,128)(2,1)S(1)} %copy.127) | copy-start | bytes 1179652
  96.3 172.6 %all-gather.8.cloned.1.call-start = ((), (), s32[]{:S(2)}) async-start(), calls=%async_computation.7 | async-start | bytes 1253376 | tf_op jit(solution)/shard_map/all_gather | solution.py:134
  101.7 73.6 %collective-permute-start.1 = (f32[2048,384]{0,1:T(8,128)}, f32[2048,384]{0,1:T(8,128)}, u32[]{:S(2)}, u32[]{:S(2)}) collective-permute-start(f32[2048,384]{0,1:T(8,128)} %add.164), channel_id=1, source_target_pairs={{0,4},{2,6},{4,0},{6,2},{8,12},{10,14},{12,8},{14,10},{16,20},{18,... | collective-permute-start | bytes 9437192 | tf_op jit(solution)/shard_map/ppermute | solution.py:150
  108.1 0.6 copy-start.5
  178.6 69.0 %collective-permute-start.2 = (f32[2048,384]{0,1:T(8,128)S(1)}, f32[2048,384]{0,1:T(8,128)}, u32[]{:S(2)}, u32[]{:S(2)}) collective-permute-start(f32[2048,384]{0,1:T(8,128)S(1)} %add.165), channel_id=1, source_target_pairs={{0,8},{2,10},{4,12},{6,14},{8,0},{10,2},{12,4},{14,6},{16,24},{18,... | collective-permute-start | bytes 9437192 | tf_op jit(solution)/shard_map/ppermute | solution.py:150
  208.0 44.4 %copy-start.7 = (f32[1,64,1,64]{3,2,1,0:T(1,128)S(1)}, f32[1,64,1,64]{3,2,1,0:T(1,128)}, u32[]{:S(2)}) copy-start(f32[1,64,1,64]{3,2,1,0:T(1,128)} %get-tuple-element.42) | copy-start | bytes 49156
  208.0 45.8 %copy-start.6 = (f32[1,64,1,64]{3,2,1,0:T(1,128)S(1)}, f32[1,64,1,64]{3,2,1,0:T(1,128)}, u32[]{:S(2)}) copy-start(f32[1,64,1,64]{3,2,1,0:T(1,128)} %get-tuple-element.41) | copy-start | bytes 49156
  251.7 136.6 %collective-permute-start.3 = (f32[2048,384]{0,1:T(8,128)}, f32[2048,384]{0,1:T(8,128)}, u32[]{:S(2)}, u32[]{:S(2)}) collective-permute-start(f32[2048,384]{0,1:T(8,128)} %add.166), channel_id=1, source_target_pairs={{0,16},{2,18},{4,20},{6,22},{8,24},{10,26},{12,28},{14,30},{16,0},... | collective-permute-start | bytes 9437192 | tf_op jit(solution)/shard_map/ppermute | solution.py:150
  265.5 3.2 copy-start.3
  267.1 1.7 copy-start.8
  388.3 8.9 %copy-start.1 = (bf16[512,2048]{1,0:T(8,128)(2,1)S(1)}, bf16[512,2048]{1,0:T(8,128)(2,1)}, u32[]{:S(2)}) copy-start(bf16[512,2048]{1,0:T(8,128)(2,1)} %param.8) | copy-start | bytes 6291460
Sparse Core Ops, SparseCore 0:
  10.3 56.5 all-gather.3
  96.4 25.2 all-gather.5
  124.0 41.0 all-gather.7
